TPU v7x, 32 devices: a whole 2x2x4 slice. The times are simulated.
32 devices in a mesh: section: 2 (over x), group: 4 (over z), narrow: 4 (over y, core).
Axes of the slice: x: 2, y: 2, z: 4, core: 2. Of those that a mesh axis runs over, the one named last changes fastest.
Arguments:
- boundary: bfloat16 [2, 8, 1024, 768], P('section', 'group', 'narrow'), may hold values from -6 to 6
- segments: int32 [8, 1024], P('group'), may hold values from 0 to 3, never falling along the last dimension, each value on 1 to 769 neighbouring positions
- qkv_weight: bfloat16 [2, 768, 2304], P('section'), may hold values from -0.21875 to 0.21875
- proj_weight: bfloat16 [2, 768, 768], P('section'), may hold values from -3 to 3
- fc1_weight: bfloat16 [2, 768, 3072], P('section'), may hold values from -0.21875 to 0.21875
- fc2_weight: bfloat16 [2, 3072, 768], P('section'), may hold values from -0.109375 to 0.109375
- gains: float32 [2, 4, 768], P('section'), may hold values from 0.5 to 1.5
- biases: float32 [2, 6, 768], P('section'), may hold values from -1.8 to 1.8
- fc1_bias: float32 [2, 3072], P('section'), may hold values from -1.8 to 1.8
Outputs:
- results: bfloat16 [2, 8, 1024, 768], P('section', 'group', 'narrow')
- grad_qkv: float32 [2, 768, 2304], P('section', 'narrow')
- grad_proj: float32 [2, 768, 768], P('section', 'narrow')
- grad_fc1: float32 [2, 768, 3072], P('section', 'narrow')
- grad_fc2: float32 [2, 3072, 768], P('section', 'narrow')
- grad_gains: float32 [2, 4, 768], P('section', None, 'narrow')
- grad_biases: float32 [2, 6, 768], P('section', None, 'narrow')
- grad_fc1_bias: float32 [2, 3072], P('section', 'narrow')
Inputs may be any that keep to these rules, and one draw needn't show every extreme that they name: `segments`: along each sequence the segment numbers never fall, every number 0 to 3 occurs, each image has 1 to 769 tokens and one image of every sequence has exactly 769.
All inputs are finite; a program needn't handle non-finite values.
Results may differ from a plain program's by a relative error of at most 0.014.
Values may be sent and summed in bfloat16 or wider, within the bound.
A program may use at most 256 MiB of HBM per device.

v0:
```python
import functools

import jax
import jax.numpy as jnp
from jax import lax
from jax.experimental import pallas as pl
from jax.experimental.pallas import tpu as pltpu
from jax.sharding import PartitionSpec as P

SECTION, GROUP, NARROW = "section", "group", "narrow"
HALVES = 2
BIG = 1e30
SLOT_ROWS = 192
SLOT_COLS = 256
RING = 6
ZRING = 8
YRING = 6
OWN_RING = 12
LENT = 5
LEND_EVERY = 5
BF = jnp.bfloat16
F32 = jnp.float32
MESH = pl.DeviceIdType.MESH


def dot_nn(left, right):
    return lax.dot_general(left, right, (((1,), (0,)), ((), ())), preferred_element_type=F32)


def dot_nt(left, right):
    return lax.dot_general(left, right, (((1,), (1,)), ((), ())), preferred_element_type=F32)


def dot_tn(left, right):
    return lax.dot_general(left, right, (((0,), (0,)), ((), ())), preferred_element_type=F32)


def aligned(start, size, unit=128):
    return pl.ds(pl.multiple_of(start, unit), size)


def norm_stats(values):
    mean = jnp.mean(values, -1, keepdims=True)
    centered = values - mean
    var = jnp.mean(centered * centered, -1, keepdims=True)
    rstd = lax.rsqrt(var + 1e-06)
    return centered * rstd, rstd


def norm_back(grad, hat, rstd, gain):
    scaled = grad * gain
    mean_one = jnp.mean(scaled, -1, keepdims=True)
    mean_two = jnp.mean(scaled * hat, -1, keepdims=True)
    return rstd * (scaled - mean_one - hat * mean_two)


def three_parts(column, lane, base):
    high = column.astype(BF).astype(F32)
    rest = column - high
    mid = rest.astype(BF).astype(F32)
    low = rest - mid
    return jnp.where(
        lane == base, high, jnp.where(lane == base + 1, mid, jnp.where(lane == base + 2, low, 0.0))
    )


def kernel(groups, *refs):
    (
        boundary, segments, wqkv_h, wproj_h, wfc1_h, wfc2_h, gains, biases, fc1b,
        results, g_qkv, g_proj, g_fc1, g_fc2, vec_out,
        wqkv, wproj, wfc1, wfc2,
        hin, cot, lhs, qaug, kall, vall, zb, rb, rhs, act, mb, fout,
        dmb, doaug, dkv_send, dkv_recv,
        segf, ckeep, csend, crecv, ysend, yrecv, rown, zsend, zrecv, ostage,
        vec, dcf, vsend, vrecv, lent,
        w_sem, b_sem, bx_sem, kv_ssem, kv_rsem, x_ssem, x_rsem, xb_ssem, xb_rsem,
        dkv_ssem, dkv_rsem, res_sem,
        c_ssem, c_rsem, y_ssem, y_rsem, z_ssem, z_rsem, o_sem,
        v_ssem, v_rsem, l_ssem, l_rsem, credit,
    ) = refs
    sec = lax.axis_index(SECTION)
    grp = lax.axis_index(GROUP)
    nar = lax.axis_index(NARROW)
    yy = nar // 2
    cc = nar % 2
    sib = (sec, grp, nar + 1 - 2 * cc)
    ynb = (sec, grp, (nar + 2) % 4)
    xnb = (1 - sec, grp, nar)
    zright = (sec, grp + 1, nar)
    zleft = (sec, grp - 1, nar)
    has_right = grp < groups - 1
    has_left = grp > 0
    is_first = sec == 0
    is_second = sec == 1

    blk = boundary.shape[2]
    rows = 2 * blk
    width = boundary.shape[3]
    ff = wfc1.shape[1]
    pairs = width // 128
    chunks = rows // blk

    n2, ob, n1 = lhs.at[0], lhs.at[1], lhs.at[2]
    gp = du = rhs.at[:, 0:ff]
    dzb, dqkv = rhs.at[:, ff : ff + width], rhs.at[:, ff + width :]
    drb, dout = rb, fout

    def bias(row):
        return biases[0:1, row * width : (row + 1) * width]

    weight_copies = [
        pltpu.make_async_copy(src.at[0], dst, w_sem.at[i])
        for i, (src, dst) in enumerate(
            ((wqkv_h, wqkv), (wproj_h, wproj), (wfc1_h, wfc1), (wfc2_h, wfc2))
        )
    ]
    for copy in weight_copies:
        copy.start()

    def own_block(dst):
        return pltpu.make_async_copy(boundary.at[0, yy], dst.at[aligned(yy * blk, blk)], b_sem)

    def swap_block(dst):
        return pltpu.make_async_remote_copy(
            src_ref=boundary.at[0, 1 - yy],
            dst_ref=dst.at[aligned(yy * blk, blk)],
            send_sem=bx_sem.at[0],
            recv_sem=bx_sem.at[1],
            device_id=ynb,
            device_id_type=MESH,
        )

    @pl.when(is_first)
    def _():
        own_block(hin).start()

    @pl.when(is_second)
    def _():
        own_block(cot).start()

    barrier = pltpu.get_barrier_semaphore()
    for peer in (sib, ynb, xnb):
        pl.semaphore_signal(barrier, inc=1, device_id=peer, device_id_type=MESH)

    @pl.when(has_right)
    def _():
        pl.semaphore_signal(barrier, inc=1, device_id=zright, device_id_type=MESH)

    @pl.when(has_left)
    def _():
        pl.semaphore_signal(barrier, inc=1, device_id=zleft, device_id_type=MESH)

    pl.semaphore_wait(barrier, 3 + has_right.astype(jnp.int32) + has_left.astype(jnp.int32))

    @pl.when(is_first)
    def _():
        swap_block(hin).start()

    @pl.when(is_second)
    def _():
        swap_block(cot).start()

    keys_seg = jnp.concatenate(
        [
            segments[pl.ds(yy, 1), aligned((half * 2 + core) * blk, blk)]
            for core in (cc, 1 - cc)
            for half in range(2)
        ],
        1,
    )
    feature = lax.rem(lax.broadcasted_iota(jnp.int32, (128, 1), 0), 64)
    hot = jnp.where(keys_seg == feature, 1.0, 0.0)
    ones = jnp.where((feature >= 4) & (feature < 7), 1.0, 0.0)
    segf[...] = jnp.where(feature < 4, hot, ones).T.astype(BF)
    vec[...] = jnp.zeros_like(vec)
    dcf[...] = jnp.zeros_like(dcf)

    lane_row = lax.broadcasted_iota(jnp.int32, (1, 128), 1)
    first_row = jnp.where(lane_row < 64, 1.0, 0.0).astype(BF)
    second_row = jnp.where(lane_row < 64, 0.0, 1.0).astype(BF)
    half_lane = lax.rem(lane_row, 64)
    penalty_row = jnp.where(half_lane < 4, BIG, 0.0)

    def x_send(dst, src, j, ssem, rsem):
        part = aligned(j * blk, blk)
        return pltpu.make_async_remote_copy(
            src_ref=src.at[part],
            dst_ref=dst.at[part],
            send_sem=ssem.at[j],
            recv_sem=rsem.at[j],
            device_id=xnb,
            device_id_type=MESH,
        )

    def kv_copy(which, j):
        ref = (kall, vall)[which]
        start = pl.multiple_of(j * blk, blk)
        return pltpu.make_async_remote_copy(
            src_ref=ref.at[pl.ds(start, blk)],
            dst_ref=ref.at[pl.ds(start + rows, blk)],
            send_sem=kv_ssem.at[which, j],
            recv_sem=kv_rsem.at[which, j],
            device_id=sib,
            device_id_type=MESH,
        )

    def project(j, carry):
        @pl.when(is_first & (j == 0))
        def _():
            own_block(hin).wait()

        @pl.when(is_first & (j > 0))
        def _():
            swap_block(hin).wait()

        @pl.when(is_second)
        def _():
            x_send(hin, fout, j, x_ssem, x_rsem).wait_recv()

        block = jnp.where(is_first, (yy + j) % 2, j)
        part = aligned(block * blk, blk)
        hat, _ = norm_stats(hin[part, :].astype(F32))
        normed = (hat * gains[0, 0:1, :] + bias(0)).astype(BF)
        n1[part, :] = normed

        @pl.when(j == 0)
        def _():
            weight_copies[0].wait()

        kall[part, :] = dot_nn(normed, wqkv[:, width : 2 * width]).astype(BF)
        kv_copy(0, block).start()
        vall[part, :] = (dot_nn(normed, wqkv[:, 2 * width :]) + bias(2)).astype(BF)
        kv_copy(1, block).start()
        low = ((dot_nn(normed, wqkv[:, 0:width]) + bias(1)).astype(BF) * 0.125).astype(F32)
        penalty = (segf[part, :].astype(F32) - 1.0) * penalty_row
        for i in range(pairs):
            pair = low[:, i * 128 : (i + 1) * 128]
            qaug[2 * i, part, :] = jnp.where(lane_row < 64, pair, penalty).astype(BF)
            qaug[2 * i + 1, part, :] = jnp.where(lane_row < 64, penalty, pair).astype(BF)
        return carry

    lax.fori_loop(0, chunks, project, 0)
    for j in range(chunks):
        kv_copy(0, j).wait()
        kv_copy(1, j).wait()

    def aug_pair(pair):
        cols = aligned(pair * 128, 128)
        keys, values, feats = kall[:, cols], vall[:, cols], segf[...]
        feat_a, feat_b = feats * second_row, feats * first_row
        return (
            (keys * first_row + feat_a, values * first_row + feat_a),
            (keys * second_row + feat_b, values * second_row + feat_b),
        )

    def feed_forward(part):
        branch = dot_nn(ob[part, :], wproj[...]) + bias(3)
        zb[part, :] = branch.astype(BF)
        middle = hin[part, :].astype(F32) + gains[0, 1:2, :] * branch
        rb[part, :] = middle
        hat, _ = norm_stats(middle)
        n2[part, :] = (hat * gains[0, 2:3, :] + bias(4)).astype(BF)

        def expand(t, carry):
            cols = aligned(t * width, width)
            pre = dot_nn(n2[part, :], wfc1[:, cols]) + fc1b[0:1, cols]
            phi = 0.5 + 0.5 * lax.erf(pre * 0.7071067811865476)
            act[part, cols] = (pre * phi).astype(BF)
            slope = phi + pre * (jnp.exp(-0.5 * pre * pre) * 0.3989422804014327)
            gp[part, cols] = slope.astype(BF)
            return carry

        lax.fori_loop(0, ff // width, expand, 0)
        mlp = dot_nn(act[part, :], wfc2[...]) + bias(5)
        mb[part, :] = mlp.astype(BF)
        fout[part, :] = (rb[part, :] + gains[0, 3:4, :] * mlp).astype(BF)

    def forward_block(j, carry):
        part = aligned(j * blk, blk)

        feats = segf[...]
        own_pen = ((segf[part, :].astype(F32) - 1.0) * penalty_row).astype(BF) * first_row

        def attend(trio, carry):
            items = [trio * 3 + i for i in range(3)]
            spans = [aligned(pair * 128, 128) for pair in items]
            scores = []
            for pair, cols in zip(items, spans):
                query = jnp.concatenate(
                    [
                        jnp.concatenate([qaug[2 * pair, part, :] * first_row, own_pen], 1),
                        jnp.concatenate([qaug[2 * pair + 1, part, :] * second_row, own_pen], 1),
                    ],
                    0,
                )
                scores.append(dot_nt(query, jnp.concatenate([kall[:, cols], feats], 1)))
            for pair, cols, score in zip(items, spans, scores):
                peak = jnp.max(score, -1, keepdims=True)
                expo = jnp.exp(score - peak).astype(BF)
                mixed = dot_nn(expo, jnp.concatenate([vall[:, cols], feats], 1))
                total = mixed[:, 132:133]
                outs = mixed[:, 0:128] / total
                log_total = peak + jnp.log(total)
                for i in range(2):
                    base = 64 * (1 - i)
                    extra = three_parts(-log_total[i * blk : (i + 1) * blk], lane_row, base + 4)
                    query = qaug[2 * pair + i, part, :]
                    qaug[2 * pair + i, part, :] = (query.astype(F32) + extra).astype(BF)
                ob[part, cols] = jnp.where(lane_row < 64, outs[:blk], outs[blk:]).astype(BF)
            return carry

        lax.fori_loop(0, pairs // 3, attend, 0)

        @pl.when(j == 0)
        def _():
            for copy in weight_copies[1:]:
                copy.wait()

        feed_forward(part)

        @pl.when(is_first)
        def _():
            x_send(hin, fout, j, x_ssem, x_rsem).start()

        return carry

    lax.fori_loop(0, chunks, forward_block, 0)

    n_fc2 = 2 * (width // 128)
    n_fc1 = ff // SLOT_COLS
    n_proj = width // SLOT_COLS
    n_qkv = 3 * width // SLOT_COLS
    lo_fc1 = n_fc2
    lo_proj = lo_fc1 + n_fc1
    lo_qkv = lo_proj + n_proj
    slots = lo_qkv + n_qkv
    mine = jnp.where(is_first, slots - LENT, slots + LENT)
    vslot = slots - LENT - 4

    def slot_at(m):
        return jnp.where(is_first, m + jnp.minimum(m // (LEND_EVERY - 1), LENT), m)

    def place_of(p):
        return jnp.where(is_first, p - jnp.minimum(p // LEND_EVERY, LENT), p)

    def is_lent(p):
        return is_first & (p % LEND_EVERY == LEND_EVERY - 1) & (p < LENT * LEND_EVERY)

    def core_copy(t):
        at = t % RING
        return pltpu.make_async_remote_copy(
            src_ref=csend.at[at], dst_ref=crecv.at[at],
            send_sem=c_ssem.at[at], recv_sem=c_rsem.at[at],
            device_id=sib, device_id_type=MESH,
        )

    def y_copy(t):
        at = t % YRING
        return pltpu.make_async_remote_copy(
            src_ref=ysend.at[at], dst_ref=yrecv.at[at],
            send_sem=y_ssem.at[at], recv_sem=y_rsem.at[at],
            device_id=ynb, device_id_type=MESH,
        )

    def z_copy(way, t):
        return pltpu.make_async_remote_copy(
            src_ref=zsend.at[way, t % RING], dst_ref=zrecv.at[way, t % ZRING],
            send_sem=z_ssem.at[way, t % RING], recv_sem=z_rsem.at[way, t % ZRING],
            device_id=(zright, zleft)[way], device_id_type=MESH,
        )

    def v_copy(stage, peer):
        return pltpu.make_async_remote_copy(
            src_ref=vsend.at[stage], dst_ref=vrecv.at[stage],
            send_sem=v_ssem.at[stage], recv_sem=v_rsem.at[stage],
            device_id=peer, device_id_type=MESH,
        )

    def lend_copy(e):
        return pltpu.make_async_remote_copy(
            src_ref=lent.at[e], dst_ref=lent.at[e],
            send_sem=l_ssem.at[e], recv_sem=l_rsem.at[e],
            device_id=xnb, device_id_type=MESH,
        )

    def give(which, t, depth, peer, count=None):
        @pl.when(t + depth < (mine if count is None else count))
        def _():
            pl.semaphore_signal(credit.at[which], inc=1, device_id=peer, device_id_type=MESH)

    def take(which, t, depth):
        @pl.when(t >= depth)
        def _():
            pl.semaphore_wait(credit.at[which], 1)

    def out_parts(p, src, act):
        @pl.when(p < lo_fc1)
        def _():
            row = (p // (width // 128)) * (2 * SLOT_ROWS)
            cols = aligned((p % (width // 128)) * 128, 128)
            for i in range(2):
                rows_of = pl.ds(pl.multiple_of(row + i * SLOT_ROWS, SLOT_ROWS), SLOT_ROWS)
                act(src.at[:, i * 128 : (i + 1) * 128], g_fc2.at[rows_of, cols], i)

        for lo, count, ref in ((lo_fc1, n_fc1, g_fc1), (lo_proj, n_proj, g_proj), (lo_qkv, n_qkv, g_qkv)):
            @pl.when((p >= lo) & (p < lo + count))
            def _():
                act(src, ref.at[:, aligned((p - lo) * SLOT_COLS, SLOT_COLS)], 0)

    def own_out(m, method):
        def act(src, dst, i):
            getattr(pltpu.make_async_copy(src, dst, o_sem.at[m % 4, i]), method)()

        out_parts(slot_at(m), ostage.at[m % 4], act)

    def lent_out(e, method):
        def act(src, dst, i):
            copy = pltpu.make_async_remote_copy(
                src_ref=src, dst_ref=dst,
                send_sem=l_ssem.at[LENT + 2 * e + i], recv_sem=l_rsem.at[LENT + 2 * e + i],
                device_id=xnb, device_id_type=MESH,
            )
            getattr(copy, method)()

        out_parts(e * LEND_EVERY + LEND_EVERY - 1, ostage.at[(slots + e) % 4], act)

    def out_start(m):
        @pl.when(m < slots)
        def _():
            own_out(m, "start")

        @pl.when(m >= slots)
        def _():
            lent_out(m - slots, "start")

    def out_wait(m):
        @pl.when(m < slots)
        def _():
            own_out(m, "wait")

        @pl.when(m >= slots)
        def _():
            lent_out(m - slots, "wait_send")

    def result_stay():
        return pltpu.make_async_copy(fout.at[aligned(yy * blk, blk)], results.at[yy], res_sem.at[0])

    def result_move():
        return pltpu.make_async_remote_copy(
            src_ref=fout.at[aligned((1 - yy) * blk, blk)], dst_ref=results.at[yy],
            send_sem=res_sem.at[1], recv_sem=res_sem.at[2],
            device_id=ynb, device_id_type=MESH,
        )

    def own_terms(q):
        @pl.when(q * 3 >= RING)
        def _():
            for i in range(3):
                core_copy(q * 3 + i - RING).wait_send()

        ring = (q % 2) * 3

        @pl.when(q < lo_fc1 // 3)
        def _():
            row = (q // 2) * (2 * SLOT_ROWS)
            cols = aligned((q % 2) * 384, 384)

            def share(dest, carry):
                got = dot_tn(act[:, aligned(dest * width + row, 2 * SLOT_ROWS)], dmb[:, cols])

                def place(ref, kind):
                    for i in range(3):
                        for half in range(2):
                            ref[ring + i, dest // 2, :, half * 128 : half * 128 + 128] = got[
                                half * SLOT_ROWS : (half + 1) * SLOT_ROWS, i * 128 : (i + 1) * 128
                            ].astype(kind)

                @pl.when(cc == dest % 2)
                def _():
                    place(ckeep, F32)

                @pl.when(cc != dest % 2)
                def _():
                    place(csend, BF)

                return carry

            lax.fori_loop(0, 4, share, 0)

        @pl.when(q >= lo_fc1 // 3)
        def _():
            cols = aligned((q * 3 - lo_fc1) * SLOT_COLS, 3 * SLOT_COLS)
            left = jnp.where(q * 3 < lo_proj, 0, jnp.where(q * 3 < lo_qkv, 1, 2))

            def share(side, carry):
                got = dot_tn(lhs[left, :, aligned(side * 2 * SLOT_ROWS, 2 * SLOT_ROWS)], rhs[:, cols])
                for core in range(2):
                    @pl.when(cc == core)
                    def _():
                        for i in range(3):
                            span = slice(i * SLOT_COLS, (i + 1) * SLOT_COLS)
                            mine, theirs = slice(0, SLOT_ROWS), slice(SLOT_ROWS, 2 * SLOT_ROWS)
                            if core:
                                mine, theirs = theirs, mine
                            ckeep[ring + i, side] = got[mine, span]
                            csend[ring + i, side] = got[theirs, span].astype(BF)

                return carry

            lax.fori_loop(0, 2, share, 0)

    def stage_own(t, carry):
        @pl.when(t % 3 == 0)
        def _():
            own_terms(t // 3)

        take(0, t, RING)
        core_copy(t).start()

        @pl.when(t == slot_at(vslot))
        def _():
            vsend[0, :, 0:width] = vec[...]
            vsend[0, :, width : width + 256] = dcf[...]
            v_copy(0, sib).start()

        return carry

    def stage_chip(p, carry):
        at = p % RING
        away = 1 - yy
        t = place_of(p)
        keeps = jnp.logical_not(is_lent(p))

        @pl.when(p < slots)
        def _():
            core_copy(p).wait_recv()

        @pl.when(keeps)
        def _():
            take(1, t, YRING)

            @pl.when(t >= YRING)
            def _():
                y_copy(t - YRING).wait_send()

            @pl.when(p < slots)
            def _():
                ysend[t % YRING] = (ckeep[at, away] + crecv[at, away].astype(F32)).astype(BF)
                rown[t % OWN_RING] = (ckeep[at, yy] + crecv[at, yy].astype(F32)).astype(BF)

            @pl.when(p >= slots)
            def _():
                lend_copy(p - slots).wait_recv()
                ysend[t % YRING] = lent[p - slots, away]
                rown[t % OWN_RING] = lent[p - slots, yy]

            y_copy(t).start()

            @pl.when(t == vslot)
            def _():
                v_copy(0, sib).wait()
                vsend[1] = vsend[0] + vrecv[0]
                v_copy(1, ynb).start()

        @pl.when(is_lent(p))
        def _():
            e = p // LEND_EVERY
            for side in range(2):
                lent[e, side] = (ckeep[at, side] + crecv[at, side].astype(F32)).astype(BF)
            lend_copy(e).start()

        @pl.when(p < slots)
        def _():
            give(0, p, RING, sib, slots)

        return carry

    def stage_group(t, carry):
        y_copy(t).wait_recv()
        at = t % OWN_RING
        rown[at] = (rown[at].astype(F32) + yrecv[t % YRING].astype(F32)).astype(BF)
        give(1, t, YRING, ynb)

        @pl.when(t == vslot)
        def _():
            v_copy(1, ynb).wait()
            vsend[2] = vsend[1] + vrecv[1]

        return carry

    def stage_line(way, t, carry):
        has_before = (has_left, has_right)[way]
        has_after = (has_right, has_left)[way]
        behind = (zleft, zright)[way]
        ahead = (zright, zleft)[way]

        @pl.when(has_before)
        def _():
            z_copy(way, t).wait_recv()

        @pl.when(has_after)
        def _():
            take(2 + way, t, ZRING)

            @pl.when(t >= RING)
            def _():
                z_copy(way, t - RING).wait_send()

            @pl.when(has_before)
            def _():
                zsend[way, t % RING] = (
                    rown[t % OWN_RING].astype(F32) + zrecv[way, t % ZRING].astype(F32)
                ).astype(BF)

            @pl.when(jnp.logical_not(has_before))
            def _():
                zsend[way, t % RING] = rown[t % OWN_RING]

            z_copy(way, t).start()

        @pl.when(t == vslot)
        def _():
            @pl.when(has_before)
            def _():
                v_copy(2 + way, behind).wait_recv()

            @pl.when(has_after)
            def _():
                @pl.when(has_before)
                def _():
                    vsend[3 + way] = vsend[2] + vrecv[2 + way]

                @pl.when(jnp.logical_not(has_before))
                def _():
                    vsend[3 + way] = vsend[2]

                v_send(way, ahead).start()

        return carry

    def stage_whole(t, carry):
        at = t % ZRING
        own = rown[t % OWN_RING].astype(F32)

        @pl.when(t >= 4)
        def _():
            out_wait(t - 4)

        @pl.when(has_left & has_right)
        def _():
            ostage[t % 4] = (own + zrecv[0, at].astype(F32) + zrecv[1, at].astype(F32)).astype(BF)

        @pl.when(has_left & jnp.logical_not(has_right))
        def _():
            ostage[t % 4] = (own + zrecv[0, at].astype(F32)).astype(BF)

        @pl.when(has_right & jnp.logical_not(has_left))
        def _():
            ostage[t % 4] = (own + zrecv[1, at].astype(F32)).astype(BF)

        out_start(t)

        @pl.when(has_left)
        def _():
            give(2, t, ZRING, zleft)

        @pl.when(has_right)
        def _():
            give(3, t, ZRING, zright)

        return carry

    def v_send(way, peer):
        return pltpu.make_async_remote_copy(
            src_ref=vsend.at[3 + way], dst_ref=vrecv.at[2 + way],
            send_sem=v_ssem.at[2 + way], recv_sem=v_rsem.at[2 + way],
            device_id=peer, device_id_type=MESH,
        )

    @pl.when(is_second)
    def _():
        result_stay().start()
        result_move().start()
        own_block(cot).wait()
        swap_block(cot).wait()

    def scale_back(j):
        part = aligned(j * blk, blk)

        @pl.when(is_first)
        def _():
            x_send(cot, dout, j, xb_ssem, xb_rsem).wait_recv()

        grad = cot[part, :].astype(F32)
        vec[3:4, :] += jnp.sum(grad * mb[part, :].astype(F32), 0, keepdims=True)
        low = (gains[0, 3:4, :] * grad).astype(BF)
        dmb[part, :] = low
        vec[9:10, :] += jnp.sum(low.astype(F32), 0, keepdims=True)

    def shrink_back(j, t):
        part = aligned(j * blk, blk)
        cols = aligned(t * width, width)
        back = dot_nt(dmb[part, :], wfc2[cols, :])
        low = (gp[part, cols].astype(F32) * back).astype(BF)
        du[part, cols] = low
        sums = jnp.sum(low.astype(F32), 0, keepdims=True)
        for i in range(width // 256):
            dcf[pl.ds(t * (width // 256) + i, 1), :] += sums[:, i * 256 : (i + 1) * 256]

    def middle_back(j):
        part = aligned(j * blk, blk)
        grad_two = dot_nt(du[part, :], wfc1[...])
        hat, rstd = norm_stats(rb[part, :])
        vec[2:3, :] += jnp.sum(grad_two * hat, 0, keepdims=True)
        vec[8:9, :] += jnp.sum(grad_two, 0, keepdims=True)
        middle = cot[part, :].astype(F32) + norm_back(grad_two, hat, rstd, gains[0, 2:3, :])
        drb[part, :] = middle
        vec[1:2, :] += jnp.sum(middle * zb[part, :].astype(F32), 0, keepdims=True)
        low = (gains[0, 1:2, :] * middle).astype(BF)
        dzb[part, :] = low
        vec[7:8, :] += jnp.sum(low.astype(F32), 0, keepdims=True)

    def heads_back(j):
        part = aligned(j * blk, blk)
        grad_o = dot_nt(dzb[part, :], wproj[...]).astype(BF).astype(F32)
        for i in range(pairs):
            cols = slice(i * 128, (i + 1) * 128)
            pair = grad_o[:, cols]
            both = pair * ob[part, cols].astype(F32)
            inner_a = jnp.sum(jnp.where(lane_row < 64, both, 0.0), -1, keepdims=True)
            inner_b = jnp.sum(jnp.where(lane_row < 64, 0.0, both), -1, keepdims=True)
            extra_a = three_parts(-inner_a, lane_row, 68)
            extra_b = three_parts(-inner_b, lane_row, 4)
            doaug[2 * i, part, :] = jnp.where(lane_row < 64, pair, extra_a).astype(BF)
            doaug[2 * i + 1, part, :] = jnp.where(lane_row < 64, extra_b, pair).astype(BF)

    def dkv_copy(index, j):
        part = aligned(j * blk, blk)
        return pltpu.make_async_remote_copy(
            src_ref=dkv_send.at[index, part],
            dst_ref=dkv_recv.at[index, part],
            send_sem=dkv_ssem.at[index, j],
            recv_sem=dkv_rsem.at[index, j],
            device_id=sib,
            device_id_type=MESH,
        )

    def quadrant(keys, values, query, outer):
        prob = jnp.exp(dot_nt(keys, query))
        diff = dot_nt(values, outer)
        slope = (prob * diff).astype(BF)
        return dot_tn(slope, keys), dot_nn(slope, query), dot_nn(prob.astype(BF), outer)

    def both_heads(parts):
        return [jnp.where(lane_row < 64, first, second) for first, second in zip(*parts)]

    def key_block(array, j):
        return jnp.concatenate([array[j * blk : (j + 1) * blk], array[rows + j * blk : rows + (j + 1) * blk]], 0)

    def pair_spans(pair):
        return [aligned(third * width + pair * 128, 128) for third in range(3)]

    def attend_back_first(pair):
        wide, narrow = [], []
        for i, (keys, values) in enumerate(aug_pair(pair)):
            query, outer = qaug[2 * pair + i], doaug[2 * pair + i]
            wide.append(quadrant(key_block(keys, 0), key_block(values, 0), query, outer))
            narrow.append(quadrant(key_block(keys, 1), key_block(values, 1), query[0:blk], outer[0:blk]))
        (dq_w, dk_w, dv_w), (dq_n, dk_n, dv_n) = both_heads(wide), both_heads(narrow)
        q_cols, k_cols, v_cols = pair_spans(pair)
        dkv_send[pair, 0:blk] = dk_w[blk:].astype(BF)
        dkv_send[pairs + pair, 0:blk] = dv_w[blk:].astype(BF)
        dkv_copy(pair, 0).start()
        dkv_copy(pairs + pair, 0).start()
        dkv_send[pair, blk:] = dk_n[blk:].astype(BF)
        dkv_send[pairs + pair, blk:] = dv_n[blk:].astype(BF)
        dqkv[0:blk, q_cols] = ((dq_w[0:blk] + dq_n) * 0.125).astype(BF)
        dqkv[blk:, q_cols] = (dq_w[blk:] * 0.125).astype(BF)
        dqkv[0:blk, k_cols] = dk_w[0:blk].astype(BF)
        dqkv[blk:, k_cols] = dk_n[0:blk].astype(BF)
        dqkv[0:blk, v_cols] = dv_w[0:blk].astype(BF)
        dqkv[blk:, v_cols] = dv_n[0:blk].astype(BF)

    def attend_back_second(duo):
        found = [second_terms(2 * duo + i) for i in range(2)]
        for i in range(2):
            second_sums(2 * duo + i, *found[i])

    def second_terms(pair):
        parts = []
        for i, (keys, values) in enumerate(aug_pair(pair)):
            query, outer = qaug[2 * pair + i, blk:], doaug[2 * pair + i, blk:]
            parts.append(quadrant(key_block(keys, 1), key_block(values, 1), query, outer))
        return both_heads(parts)

    def second_sums(pair, dq, dk, dv):
        q_cols, k_cols, v_cols = pair_spans(pair)
        for index, term in ((pair, dk), (pairs + pair, dv)):
            dkv_send[index, blk:] = (dkv_send[index, blk:].astype(F32) + term[blk:]).astype(BF)
            dkv_copy(index, 1).start()
        for cols, term in ((q_cols, dq * 0.125), (k_cols, dk[0:blk]), (v_cols, dv[0:blk])):
            dqkv[blk:, cols] = (dqkv[blk:, cols].astype(F32) + term).astype(BF)

    def finish_back(j):
        part = aligned(j * blk, blk)

        def collect(index, carry):
            dkv_copy(index, j).wait()
            cols = aligned(width + index * 128, 128)
            dqkv[part, cols] = (dqkv[part, cols].astype(F32) + dkv_recv[index, part].astype(F32)).astype(BF)
            return carry

        lax.fori_loop(0, 2 * pairs, collect, 0)

        @pl.when(is_first & (j == 0))
        def _():
            for i in range(chunks):
                x_send(hin, fout, i, x_ssem, x_rsem).wait_send()

        @pl.when(is_second & (j == 0))
        def _():
            result_stay().wait()
            result_move().wait_send()

        vec[5:6, :] += jnp.sum(dqkv[part, 0:width].astype(F32), 0, keepdims=True)
        vec[6:7, :] += jnp.sum(dqkv[part, 2 * width : 3 * width].astype(F32), 0, keepdims=True)
        grad_one = dot_nt(dqkv[part, :], wqkv[...])
        hat, rstd = norm_stats(hin[part, :].astype(F32))
        vec[0:1, :] += jnp.sum(grad_one * hat, 0, keepdims=True)
        vec[4:5, :] += jnp.sum(grad_one, 0, keepdims=True)
        total = drb[part, :] + norm_back(grad_one, hat, rstd, gains[0, 0:1, :])
        dout[part, :] = total.astype(BF)

        @pl.when(is_second)
        def _():
            x_send(cot, dout, j, xb_ssem, xb_rsem).start()

    tiles = ff // width
    per_block = tiles + 3
    dense = chunks * per_block
    first_end = dense + pairs
    second_end = first_end + 1 + pairs // 2

    beside = 22

    def pieces_done(v):
        total = second_end + 1
        first = per_block + 1
        spread = jnp.minimum(first + (v * (total - first) + beside - 1) // beside, total)
        return jnp.where(v < 0, 0, jnp.where(is_first, spread, total))

    def advance(stage, lag, count, v, at=lambda m: m):
        def done(v):
            return jnp.minimum(jnp.maximum(v + 1 - lag, 0), count)

        lax.fori_loop(at(done(v - 1)), at(done(v)), stage, 0)

    late = jnp.maximum(grp, groups - 1 - grp)
    chip_lag, group_lag, hop_lag = 2, 4, 2
    visits = mine + group_lag + hop_lag * (groups - 1)

    def piece(w, carry):
        @pl.when(w < dense)
        def _():
            j, r = w // per_block, w % per_block

            @pl.when(r == 0)
            def _():
                scale_back(j)

            @pl.when((r > 0) & (r <= tiles))
            def _():
                shrink_back(j, r - 1)

            @pl.when(r == tiles + 1)
            def _():
                middle_back(j)

            @pl.when(r == tiles + 2)
            def _():
                heads_back(j)

        @pl.when((w >= dense) & (w < first_end))
        def _():
            attend_back_first(w - dense)

        @pl.when((w > first_end) & (w < second_end))
        def _():
            attend_back_second(w - first_end - 1)

        @pl.when((w == first_end) | (w == second_end))
        def _():
            finish_back((w - first_end) // (pairs // 2 + 1))

        return carry

    def visit(v, carry):
        lax.fori_loop(pieces_done(v - 1), pieces_done(v), piece, 0)
        advance(stage_own, 0, jnp.minimum(mine, slots), v, slot_at)
        advance(stage_chip, chip_lag, mine, v, slot_at)
        advance(stage_group, group_lag, mine, v)
        for way in range(2):
            place = grp if way == 0 else groups - 1 - grp
            advance(functools.partial(stage_line, way), group_lag + hop_lag * place, mine, v)
        advance(stage_whole, group_lag + hop_lag * late, mine, v)

        @pl.when(is_first & (v == slots))
        def _():
            result_stay().start()
            result_move().start()

        return carry

    lax.fori_loop(0, visits, visit, 0)

    def drain(i, carry):
        y_copy(mine - YRING + i).wait_send()

        @pl.when(i < 4)
        def _():
            out_wait(mine - 4 + i)

        @pl.when(i < RING)
        def _():
            core_copy(slots - RING + i).wait_send()

            @pl.when(has_right)
            def _():
                z_copy(0, mine - RING + i).wait_send()

            @pl.when(has_left)
            def _():
                z_copy(1, mine - RING + i).wait_send()

        return carry

    lax.fori_loop(0, YRING, drain, 0)

    @pl.when(is_first)
    def _():
        for e in range(LENT):
            lend_copy(e).wait_send()
            lent_out(e, "wait_recv")

    @pl.when(has_right)
    def _():
        v_send(0, zright).wait_send()

    @pl.when(has_left)
    def _():
        v_send(1, zleft).wait_send()

    total = vsend[2]
    vec_out[...] = total

    @pl.when(has_left)
    def _():
        vec_out[...] = vec_out[...] + vrecv[2]

    @pl.when(has_right)
    def _():
        vec_out[...] = vec_out[...] + vrecv[3]

    @pl.when(is_first)
    def _():
        result_stay().wait()
        result_move().wait_send()

    @pl.when(is_second)
    def _():
        for j in range(chunks):
            x_send(cot, dout, j, xb_ssem, xb_rsem).wait_send()

    result_move().wait_recv()

HEADS = 12
HDIM = 64


def from_behind(block, axis, distance):
    devices = range(lax.axis_size(axis))
    route = [(i - distance, i) for i in devices if i - distance in devices]
    return lax.ppermute(block, axis, route)


def normalize(values, scale_vec, shift_vec):
    row_mean = jnp.mean(values, -1, keepdims=True)
    centered = values - row_mean
    variance = jnp.mean(centered * centered, -1, keepdims=True)
    return centered * lax.rsqrt(variance + 1e-06) * scale_vec + shift_vec


def gelu_exact(values):
    return jax.nn.gelu(values, approximate=False)


def back_dot(left, weight):
    return lax.dot_general(
        left, weight, (((1,), (1,)), ((), ())), preferred_element_type=jnp.float32
    )


def row_contract(left, right):
    return lax.dot_general(
        left, right, (((0,), (0,)), ((), ())), preferred_element_type=jnp.float32
    )


def masked_scores(query, keys_all, seg_row):
    row_count = query.shape[0]
    length = keys_all.shape[0]
    start = lax.axis_index("narrow") * row_count
    own_seg = lax.dynamic_slice_in_dim(seg_row, start, row_count)
    same = own_seg[:, None] == seg_row[None, :]
    raw = (
        jnp.einsum(
            "qhd,khd->hqk",
            query.reshape(row_count, HEADS, HDIM),
            keys_all.reshape(length, HEADS, HDIM),
            preferred_element_type=jnp.float32,
        )
        * 0.125
    )
    return jnp.where(same[None], raw, -1e30)


def forward_layer(inputs, seg_row, weights):
    qkv_w, proj_w, fc1_w, fc2_w, gain_rows, bias_rows, fc1_b = weights
    row_count, model_width = inputs.shape
    normed = normalize(inputs, gain_rows[0], bias_rows[0]).astype(jnp.bfloat16)
    qkv = jnp.dot(normed, qkv_w, preferred_element_type=jnp.float32)
    query = (qkv[:, :model_width] + bias_rows[1]).astype(jnp.bfloat16)
    key_rows = qkv[:, model_width : 2 * model_width].astype(jnp.bfloat16)
    value_rows = (qkv[:, 2 * model_width :] + bias_rows[2]).astype(jnp.bfloat16)
    keys_all, values_all = (
        lax.all_gather(key_rows, "narrow", axis=0, tiled=True),
        lax.all_gather(value_rows, "narrow", axis=0, tiled=True),
    )
    length = keys_all.shape[0]
    scores = masked_scores(query, keys_all, seg_row)
    peak = jnp.max(scores, -1, keepdims=True)
    log_total = peak + jnp.log(jnp.sum(jnp.exp(scores - peak), -1, keepdims=True))
    probs = jnp.exp(scores - log_total).astype(jnp.bfloat16)
    mixed = jnp.einsum(
        "hqk,khd->qhd",
        probs,
        values_all.reshape(length, HEADS, HDIM),
        preferred_element_type=jnp.float32,
    )
    attended = mixed.reshape(row_count, model_width).astype(jnp.bfloat16)
    branch = jnp.dot(attended, proj_w, preferred_element_type=jnp.float32) + bias_rows[3]
    middle = inputs + gain_rows[1] * branch
    normed_two = normalize(middle, gain_rows[2], bias_rows[4]).astype(jnp.bfloat16)
    hidden_pre = jnp.dot(normed_two, fc1_w, preferred_element_type=jnp.float32) + fc1_b
    activated = gelu_exact(hidden_pre).astype(jnp.bfloat16)
    mlp_out = jnp.dot(activated, fc2_w, preferred_element_type=jnp.float32) + bias_rows[5]
    output = middle + gain_rows[3] * mlp_out
    saved = (
        inputs,
        query,
        keys_all,
        values_all,
        log_total,
        attended,
        branch,
        middle,
        hidden_pre,
        mlp_out,
    )
    return (output, saved)


def backward_layer(grad_out, saved, seg_row, weights):
    qkv_w, proj_w, fc1_w, fc2_w, gain_rows, bias_rows, fc1_b = weights
    (
        inputs,
        query,
        keys_all,
        values_all,
        log_total,
        attended,
        branch,
        middle,
        hidden_pre,
        mlp_out,
    ) = saved
    row_count, model_width = inputs.shape
    length = keys_all.shape[0]
    scale_two = jnp.sum(grad_out * mlp_out, 0)
    mlp_grad = (gain_rows[3] * grad_out).astype(jnp.bfloat16)
    activated, gelu_pull = jax.vjp(gelu_exact, hidden_pre)
    grad_fc2 = row_contract(activated.astype(jnp.bfloat16), mlp_grad)
    shift_five = jnp.sum(mlp_grad.astype(jnp.float32), 0)
    pre_grad = gelu_pull(back_dot(mlp_grad, fc2_w))[0].astype(jnp.bfloat16)
    normed_two, norm_pull_two = jax.vjp(normalize, middle, gain_rows[2], bias_rows[4])
    grad_fc1 = row_contract(normed_two.astype(jnp.bfloat16), pre_grad)
    grad_fc1b = jnp.sum(pre_grad.astype(jnp.float32), 0)
    middle_part, gain_two, shift_four = norm_pull_two(back_dot(pre_grad, fc1_w))
    middle_grad = grad_out + middle_part
    scale_one = jnp.sum(middle_grad * branch, 0)
    branch_grad = (gain_rows[1] * middle_grad).astype(jnp.bfloat16)
    grad_proj = row_contract(attended, branch_grad)
    shift_three = jnp.sum(branch_grad.astype(jnp.float32), 0)
    heads_grad = back_dot(branch_grad, proj_w).astype(jnp.bfloat16).reshape(row_count, HEADS, HDIM)
    scores = masked_scores(query, keys_all, seg_row)
    probs = jnp.exp(scores - log_total)
    keys_heads = keys_all.reshape(length, HEADS, HDIM)
    prob_grad = jnp.einsum(
        "qhd,khd->hqk",
        heads_grad,
        values_all.reshape(length, HEADS, HDIM),
        preferred_element_type=jnp.float32,
    )
    inner = jnp.sum(probs * prob_grad, -1, keepdims=True)
    score_grad = (probs * (prob_grad - inner)).astype(jnp.bfloat16)
    query_grad = (
        (
            jnp.einsum("hqk,khd->qhd", score_grad, keys_heads, preferred_element_type=jnp.float32)
            * 0.125
        )
        .reshape(row_count, model_width)
        .astype(jnp.bfloat16)
    )
    key_part = (
        jnp.einsum(
            "hqk,qhd->khd",
            score_grad,
            query.reshape(row_count, HEADS, HDIM),
            preferred_element_type=jnp.float32,
        )
        * 0.125
    ).reshape(length, model_width)
    value_part = jnp.einsum(
        "hqk,qhd->khd", probs.astype(jnp.bfloat16), heads_grad, preferred_element_type=jnp.float32
    ).reshape(length, model_width)
    key_sum, value_sum = (
        lax.psum_scatter(
            key_part.astype(jnp.bfloat16), "narrow", scatter_dimension=0, tiled=True
        ).astype(jnp.float32),
        lax.psum_scatter(
            value_part.astype(jnp.bfloat16), "narrow", scatter_dimension=0, tiled=True
        ).astype(jnp.float32),
    )
    key_grad = key_sum.astype(jnp.bfloat16)
    value_grad = value_sum.astype(jnp.bfloat16)
    qkv_grad = jnp.concatenate([query_grad, key_grad, value_grad], 1)
    normed, norm_pull_one = jax.vjp(normalize, inputs, gain_rows[0], bias_rows[0])
    grad_qkv = row_contract(normed.astype(jnp.bfloat16), qkv_grad)
    input_part, gain_one, shift_zero = norm_pull_one(back_dot(qkv_grad, qkv_w))
    input_grad = middle_grad + input_part
    gain_grads = jnp.stack([gain_one, scale_one, gain_two, scale_two])
    shift_grads = jnp.stack(
        [
            shift_zero,
            jnp.sum(query_grad.astype(jnp.float32), 0),
            jnp.sum(value_grad.astype(jnp.float32), 0),
            shift_three,
            shift_four,
            shift_five,
        ]
    )
    return (
        input_grad,
        (grad_qkv, grad_proj, grad_fc1, grad_fc2, gain_grads, shift_grads, grad_fc1b),
    )


def general_body(
    boundary, segments, qkv_weight, proj_weight, fc1_weight, fc2_weight, gains, biases, fc1_bias
):
    weights = (
        qkv_weight[0],
        proj_weight[0],
        fc1_weight[0],
        fc2_weight[0],
        gains[0],
        biases[0],
        fc1_bias[0],
    )
    local_ends = boundary[0]
    micro_count = local_ends.shape[0]
    first_section = lax.axis_index("section") == 0
    arrived = jnp.zeros(local_ends.shape[1:], jnp.bfloat16)
    stored = []
    outputs = []
    for step_index in range(micro_count + 1):
        lower = min(step_index, micro_count - 1)
        upper = max(step_index - 1, 0)
        inputs = jnp.where(
            first_section, local_ends[lower].astype(jnp.float32), arrived.astype(jnp.float32)
        )
        seg_row = jnp.where(first_section, segments[lower], segments[upper])
        output, saved = forward_layer(inputs, seg_row, weights)
        stored.append((saved, seg_row))
        outputs.append(output)
        if step_index < micro_count:
            arrived = from_behind(output.astype(jnp.bfloat16), "section", 1)
    totals = tuple((jnp.zeros(w.shape, jnp.float32) for w in weights))
    returned = jnp.zeros(local_ends.shape[1:], jnp.bfloat16)
    input_grads = []
    for step_index in range(micro_count + 1):
        lower = min(step_index, micro_count - 1)
        upper = max(step_index - 1, 0)
        picked = jax.tree.map(
            lambda early, later: jnp.where(first_section, early, later),
            stored[upper],
            stored[lower + 1],
        )
        cotangent = jnp.where(
            first_section, returned.astype(jnp.float32), local_ends[lower].astype(jnp.float32)
        )
        is_valid = jnp.where(first_section, step_index >= 1, step_index < micro_count)
        cotangent = jnp.where(is_valid, cotangent, 0.0)
        grad_in, pieces = backward_layer(cotangent, picked[0], picked[1], weights)
        totals = tuple((acc + part for acc, part in zip(totals, pieces)))
        input_grads.append(grad_in)
        if step_index < micro_count:
            returned = from_behind(grad_in.astype(jnp.bfloat16), "section", -1)
    results = jnp.stack(
        [jnp.where(first_section, input_grads[j + 1], outputs[j + 1]) for j in range(micro_count)]
    )
    results = results.astype(jnp.bfloat16)
    within = (
        lax.psum_scatter(
            totals[0].astype(jnp.bfloat16), "narrow", scatter_dimension=0, tiled=True
        ).astype(jnp.float32),
        lax.psum_scatter(
            totals[1].astype(jnp.bfloat16), "narrow", scatter_dimension=0, tiled=True
        ).astype(jnp.float32),
        lax.psum_scatter(
            totals[2].astype(jnp.bfloat16), "narrow", scatter_dimension=0, tiled=True
        ).astype(jnp.float32),
        lax.psum_scatter(
            totals[3].astype(jnp.bfloat16), "narrow", scatter_dimension=0, tiled=True
        ).astype(jnp.float32),
        lax.psum_scatter(
            totals[4].astype(jnp.bfloat16), "narrow", scatter_dimension=1, tiled=True
        ).astype(jnp.float32),
        lax.psum_scatter(
            totals[5].astype(jnp.bfloat16), "narrow", scatter_dimension=1, tiled=True
        ).astype(jnp.float32),
        lax.psum_scatter(
            totals[6].astype(jnp.bfloat16), "narrow", scatter_dimension=0, tiled=True
        ).astype(jnp.float32),
    )
    final = (
        lax.psum(within[0].astype(jnp.bfloat16), "group").astype(jnp.float32),
        lax.psum(within[1].astype(jnp.bfloat16), "group").astype(jnp.float32),
        lax.psum(within[2].astype(jnp.bfloat16), "group").astype(jnp.float32),
        lax.psum(within[3].astype(jnp.bfloat16), "group").astype(jnp.float32),
        lax.psum(within[4].astype(jnp.bfloat16), "group").astype(jnp.float32),
        lax.psum(within[5].astype(jnp.bfloat16), "group").astype(jnp.float32),
        lax.psum(within[6].astype(jnp.bfloat16), "group").astype(jnp.float32),
    )
    return (
        results[None],
        final[0][None],
        final[1][None],
        final[2][None],
        final[3][None],
        final[4][None],
        final[5][None],
        final[6][None],
    )


def fused_body(
    groups, boundary, segments, qkv_weight, proj_weight, fc1_weight, fc2_weight, gains, biases, fc1_bias
):
    blk, width = boundary.shape[2:]
    rows, keys = 2 * blk, 4 * blk
    ff = fc1_weight.shape[2]
    heads = width // HDIM
    nar = lax.axis_index(NARROW)

    def bf(*shape):
        return pltpu.VMEM(shape, BF)

    def f32(*shape):
        return pltpu.VMEM(shape, F32)

    dma = pltpu.SemaphoreType.DMA
    slot = (SLOT_ROWS, SLOT_COLS)
    scratch = [
        bf(width, 3 * width), bf(width, width), bf(width, ff), bf(ff, width),
        bf(rows, width), bf(rows, width), bf(3, rows, width), bf(heads, rows, 128),
        bf(keys, width), bf(keys, width), bf(rows, width), f32(rows, width),
        bf(rows, ff + 4 * width), bf(rows, ff), bf(rows, width), bf(rows, width),
        bf(rows, width), bf(heads, rows, 128), bf(heads, rows, 128), bf(heads, rows, 128),
        bf(keys, 128), f32(RING, 2, *slot), bf(RING, 2, *slot), bf(RING, 2, *slot),
        bf(YRING, *slot), bf(YRING, *slot), bf(OWN_RING, *slot), bf(2, RING, *slot), bf(2, ZRING, *slot), bf(4, *slot),
        f32(16, width), f32(16, 256), f32(5, 16, width + 256), f32(4, 16, width + 256), bf(LENT, 2, *slot),
        dma((4,)), dma(()), dma((2,)), dma((2, 2)), dma((2, 2)), dma((2,)), dma((2,)), dma((2,)), dma((2,)),
        dma((heads, 2)), dma((heads, 2)), dma((3,)),
        dma((RING,)), dma((RING,)), dma((YRING,)), dma((YRING,)), dma((2, RING)), dma((2, ZRING)), dma((4, 2)),
        dma((4,)), dma((4,)), dma((3 * LENT,)), dma((3 * LENT,)), pltpu.SemaphoreType.REGULAR((4,)),
    ]
    hbm = pl.BlockSpec(memory_space=pl.ANY)
    vmem = pl.BlockSpec(memory_space=pltpu.VMEM)
    out = pl.pallas_call(
        functools.partial(kernel, groups),
        out_shape=(
            jax.ShapeDtypeStruct((2, blk, width), BF),
            jax.ShapeDtypeStruct((width // 4, 3 * width), BF),
            jax.ShapeDtypeStruct((width // 4, width), BF),
            jax.ShapeDtypeStruct((width // 4, ff), BF),
            jax.ShapeDtypeStruct((ff // 4, width), BF),
            jax.ShapeDtypeStruct((16, width + 256), F32),
        ),
        in_specs=[hbm, vmem, hbm, hbm, hbm, hbm, vmem, vmem, vmem],
        out_specs=(hbm, hbm, hbm, hbm, hbm, vmem),
        scratch_shapes=scratch,
        compiler_params=pltpu.CompilerParams(
            collective_id=0, has_side_effects=True, vmem_limit_bytes=63 * 2**20
        ),
        name="two_layers",
    )(boundary, segments, qkv_weight, proj_weight, fc1_weight, fc2_weight, gains, biases.reshape(1, -1), fc1_bias)
    results, qkv, proj, fc1, fc2, vecs = out
    return widen(results, qkv, proj, fc1, fc2, vecs)


def widen_kernel(results, qkv, proj, fc1, fc2, vecs, *outs):
    o_results, o_qkv, o_proj, o_fc1, o_fc2, o_gains, o_biases, o_fc1b = outs
    o_results[0] = results[...]
    for src, dst in ((qkv, o_qkv), (proj, o_proj), (fc1, o_fc1), (fc2, o_fc2)):
        dst[0] = src[...].astype(F32)

    @pl.when(pl.program_id(0) == 0)
    def _():
        nar = lax.axis_index(NARROW)
        share = o_gains.shape[2]
        parts = o_fc1b.shape[1] // 256
        for i in range(4):
            @pl.when(nar == i)
            def _():
                cols = slice(i * share, (i + 1) * share)
                o_gains[0] = vecs[0:4, cols]
                for row in range(6):
                    o_biases[row] = vecs[4 + row : 5 + row, cols]
                for part in range(parts):
                    o_fc1b[:, part * 256 : (part + 1) * 256] = vecs[
                        i * parts + part : i * parts + part + 1, 4 * share :
                    ]


def widen(results, qkv, proj, fc1, fc2, vecs):
    steps = 4

    def block(shape, lead):
        size = (shape[0] // steps,) + shape[1:]
        rest = (0,) * (len(shape) - 1)
        if lead:
            return pl.BlockSpec((1,) + size, lambda i: (0, i) + rest)
        return pl.BlockSpec(size, lambda i: (i,) + rest)

    def whole(shape):
        return pl.BlockSpec(shape, lambda i: (0,) * len(shape))

    halves, rows, width = results.shape
    flat = results.reshape(halves * rows, width)
    flats = (flat, qkv, proj, fc1, fc2)
    share = width // 4
    small = ((1, 4, share), (6, 1, share), (1, fc2.shape[0]))
    out = pl.pallas_call(
        widen_kernel,
        grid=(steps,),
        in_specs=[block(a.shape, False) for a in flats] + [whole(vecs.shape)],
        out_specs=[block(a.shape, True) for a in flats] + [whole(s) for s in small],
        out_shape=[jax.ShapeDtypeStruct((1,) + a.shape, BF if i == 0 else F32) for i, a in enumerate(flats)]
        + [jax.ShapeDtypeStruct(s, F32) for s in small],
        name="widen",
    )(*flats, vecs)
    return (
        out[0].reshape(1, halves, rows, width),
        *out[1:6],
        out[6].transpose(1, 0, 2),
        out[7],
    )


def solution(mesh):
    sections, groups, narrow = (mesh.shape[name] for name in (SECTION, GROUP, NARROW))
    placed = (
        P("section", "group", "narrow", None),
        P("group", None),
        P("section", None, None),
        P("section", None, None),
        P("section", None, None),
        P("section", None, None),
        P("section", None, None),
        P("section", None, None),
        P("section", None),
    )
    fused = sections == 2 and narrow == 4 and groups > 1
    body = functools.partial(fused_body, groups) if fused else general_body
    return jax.shard_map(
        body,
        mesh=mesh,
        in_specs=placed,
        out_specs=(
            P("section", "group", "narrow", None),
            P("section", "narrow", None),
            P("section", "narrow", None),
            P("section", "narrow", None),
            P("section", "narrow", None),
            P("section", None, "narrow"),
            P("section", None, "narrow"),
            P("section", "narrow"),
        ),
        check_vma=False,
    )
```

profile of v0, /device:TPU:0, one launch (start us, length us, event | category | flops | bytes accessed | tf_op | source)
XLA Modules:
  0.0 237.5 jit_solution(8029818177709424844)
XLA Ops:
  0.6 230.7 %two_layers.1 = (bf16[2,256,768]{2,1,0:T(8,128)(2,1)}, bf16[192,2304]{1,0:T(8,128)(2,1)}, bf16[192,768]{1,0:T(8,128)(2,1)}, bf16[192,3072]{1,0:T(8,128)(2,1)}, b...) custom-call(bf16[1,2,256,768]{3,2,1,0:T(8,128)(2,1)} %refs_0_.1, s32[2,1024]{1,0:T(2,128)} %refs_1_.1, ...), custom_call_target="tpu_custom_call" | custom-call | tf_op jit(solution)/shard_map/two_layers/pallas_call | solution.py:1300
  231.4 6.0 %widen.1 = (bf16[1,512,768]{2,1,0:T(8,128)(2,1)}, f32[1,192,2304]{2,1,0:T(8,128)}, f32[1,192,768]{2,1,0:T(8,128)}, f32[1,192,3072]{2,1,0:T(8,128)}, f32[1,768,76...) custom-call(bf16[512,768]{1,0:T(8,128)(2,1)} %bitcast.4, ...), custom_call_target="tpu_custom_call" | custom-call | tf_op jit(solution)/shard_map/widen/pallas_call | solution.py:1364
where the time goes:
time: 238 us
  Pallas kernels  237 us (100%)
    pallas_call x1, Pallas kernels, fused_body(): pl.pallas_call(functools.partial(kernel, groups), out_shape=(jax.ShapeDty...  231 us
    pallas_call x1, Pallas kernels, widen(): pl.pallas_call(widen_kernel, grid=(steps,), in_specs=[block(a.shape, Fals...  6.03 us

commit v1 on v0

--- a/solution.py
+++ b/solution.py
@@ -120,12 +120,14 @@
     def own_block(dst):
         return pltpu.make_async_copy(boundary.at[0, yy], dst.at[aligned(yy * blk, blk)], b_sem)
 
-    def swap_block(dst):
+    half_blk = blk // 2
+
+    def swap_half(dst, half):
         return pltpu.make_async_remote_copy(
-            src_ref=boundary.at[0, 1 - yy],
-            dst_ref=dst.at[aligned(yy * blk, blk)],
-            send_sem=bx_sem.at[0],
-            recv_sem=bx_sem.at[1],
+            src_ref=boundary.at[0, 1 - yy, pl.ds(half * half_blk, half_blk)],
+            dst_ref=dst.at[aligned(yy * blk + half * half_blk, half_blk)],
+            send_sem=bx_sem.at[0, half],
+            recv_sem=bx_sem.at[1, half],
             device_id=ynb,
             device_id_type=MESH,
         )
@@ -154,11 +156,13 @@
 
     @pl.when(is_first)
     def _():
-        swap_block(hin).start()
+        swap_half(hin, 0).start()
+        swap_half(hin, 1).start()
 
     @pl.when(is_second)
     def _():
-        swap_block(cot).start()
+        swap_half(cot, 0).start()
+        swap_half(cot, 1).start()
 
     keys_seg = jnp.concatenate(
         [
@@ -192,66 +196,74 @@
             device_id_type=MESH,
         )
 
-    def kv_copy(which, j):
+    def x_half(half):
+        part = aligned((chunks - 1) * blk + half * half_blk, half_blk)
+        return pltpu.make_async_remote_copy(
+            src_ref=fout.at[part],
+            dst_ref=hin.at[part],
+            send_sem=x_ssem.at[chunks - 1 + half],
+            recv_sem=x_rsem.at[chunks - 1 + half],
+            device_id=xnb,
+            device_id_type=MESH,
+        )
+
+    def kv_copy(which, part):
         ref = (kall, vall)[which]
-        start = pl.multiple_of(j * blk, blk)
+        index = part.start // half_blk
         return pltpu.make_async_remote_copy(
-            src_ref=ref.at[pl.ds(start, blk)],
-            dst_ref=ref.at[pl.ds(start + rows, blk)],
-            send_sem=kv_ssem.at[which, j],
-            recv_sem=kv_rsem.at[which, j],
+            src_ref=ref.at[part],
+            dst_ref=ref.at[aligned(part.start + rows, part.size)],
+            send_sem=kv_ssem.at[which, index],
+            recv_sem=kv_rsem.at[which, index],
             device_id=sib,
             device_id_type=MESH,
         )
 
-    def project(j, carry):
-        @pl.when(is_first & (j == 0))
-        def _():
-            own_block(hin).wait()
-
-        @pl.when(is_first & (j > 0))
-        def _():
-            swap_block(hin).wait()
-
-        @pl.when(is_second)
-        def _():
-            x_send(hin, fout, j, x_ssem, x_rsem).wait_recv()
-
-        block = jnp.where(is_first, (yy + j) % 2, j)
-        part = aligned(block * blk, blk)
+    def project(part):
+        size = part.size
         hat, _ = norm_stats(hin[part, :].astype(F32))
         normed = (hat * gains[0, 0:1, :] + bias(0)).astype(BF)
         n1[part, :] = normed
-
-        @pl.when(j == 0)
-        def _():
-            weight_copies[0].wait()
-
         kall[part, :] = dot_nn(normed, wqkv[:, width : 2 * width]).astype(BF)
-        kv_copy(0, block).start()
+        kv_copy(0, part).start()
         vall[part, :] = (dot_nn(normed, wqkv[:, 2 * width :]) + bias(2)).astype(BF)
-        kv_copy(1, block).start()
+        kv_copy(1, part).start()
         low = ((dot_nn(normed, wqkv[:, 0:width]) + bias(1)).astype(BF) * 0.125).astype(F32)
         penalty = (segf[part, :].astype(F32) - 1.0) * penalty_row
         for i in range(pairs):
             pair = low[:, i * 128 : (i + 1) * 128]
             qaug[2 * i, part, :] = jnp.where(lane_row < 64, pair, penalty).astype(BF)
             qaug[2 * i + 1, part, :] = jnp.where(lane_row < 64, penalty, pair).astype(BF)
+
+    @pl.when(is_first)
+    def _():
+        own_block(hin).wait()
+
+    @pl.when(is_second)
+    def _():
+        x_send(hin, fout, 0, x_ssem, x_rsem).wait_recv()
+
+    weight_copies[0].wait()
+    first_at = jnp.where(is_first, yy, 0) * blk
+    project(aligned(first_at, blk))
+
+    def project_half(half, carry):
+        @pl.when(is_first)
+        def _():
+            swap_half(hin, half).wait()
+
+        @pl.when(is_second)
+        def _():
+            x_half(half).wait_recv()
+
+        project(aligned(blk - first_at + half * half_blk, half_blk))
         return carry
 
-    lax.fori_loop(0, chunks, project, 0)
-    for j in range(chunks):
-        kv_copy(0, j).wait()
-        kv_copy(1, j).wait()
-
-    def aug_pair(pair):
-        cols = aligned(pair * 128, 128)
-        keys, values, feats = kall[:, cols], vall[:, cols], segf[...]
-        feat_a, feat_b = feats * second_row, feats * first_row
-        return (
-            (keys * first_row + feat_a, values * first_row + feat_a),
-            (keys * second_row + feat_b, values * second_row + feat_b),
-        )
+    lax.fori_loop(0, 2, project_half, 0)
+    for which in range(2):
+        kv_copy(which, aligned(first_at, blk)).wait()
+        for half in range(2):
+            kv_copy(which, aligned(blk - first_at + half * half_blk, half_blk)).wait()
 
     def feed_forward(part):
         branch = dot_nn(ob[part, :], wproj[...]) + bias(3)
@@ -270,7 +282,7 @@
             gp[part, cols] = slope.astype(BF)
             return carry
 
-        lax.fori_loop(0, ff // width, expand, 0)
+        lax.fori_loop(0, ff // width, expand, 0, unroll=True)
         mlp = dot_nn(act[part, :], wfc2[...]) + bias(5)
         mb[part, :] = mlp.astype(BF)
         fout[part, :] = (rb[part, :] + gains[0, 3:4, :] * mlp).astype(BF)
@@ -309,16 +321,27 @@
                 ob[part, cols] = jnp.where(lane_row < 64, outs[:blk], outs[blk:]).astype(BF)
             return carry
 
-        lax.fori_loop(0, pairs // 3, attend, 0)
+        lax.fori_loop(0, pairs // 3, attend, 0, unroll=True)
 
         @pl.when(j == 0)
         def _():
             for copy in weight_copies[1:]:
                 copy.wait()
 
-        feed_forward(part)
-
-        @pl.when(is_first)
+        @pl.when(is_first & (j == chunks - 1))
+        def _():
+            def feed_half(half, carry):
+                feed_forward(aligned((chunks - 1) * blk + half * half_blk, half_blk))
+                x_half(half).start()
+                return carry
+
+            lax.fori_loop(0, 2, feed_half, 0)
+
+        @pl.when(is_second | (j < chunks - 1))
+        def _():
+            feed_forward(part)
+
+        @pl.when(is_first & (j < chunks - 1))
         def _():
             x_send(hin, fout, j, x_ssem, x_rsem).start()
 
@@ -336,12 +359,22 @@
     slots = lo_qkv + n_qkv
     mine = jnp.where(is_first, slots - LENT, slots + LENT)
     vslot = slots - LENT - 4
+    lent_from = slots - LENT - 1
 
     def slot_at(m):
         return jnp.where(is_first, m + jnp.minimum(m // (LEND_EVERY - 1), LENT), m)
 
     def place_of(p):
         return jnp.where(is_first, p - jnp.minimum(p // LEND_EVERY, LENT), p)
+
+    def lent_before(m):
+        return jnp.minimum(jnp.maximum(m - lent_from, 0), LENT)
+
+    def own_slot(m):
+        return jnp.where(is_first, slot_at(m), m - lent_before(m))
+
+    def is_borrowed(m):
+        return is_second & (m >= lent_from) & (m < lent_from + LENT)
 
     def is_lent(p):
         return is_first & (p % LEND_EVERY == LEND_EVERY - 1) & (p < LENT * LEND_EVERY)
@@ -411,7 +444,7 @@
         def act(src, dst, i):
             getattr(pltpu.make_async_copy(src, dst, o_sem.at[m % 4, i]), method)()
 
-        out_parts(slot_at(m), ostage.at[m % 4], act)
+        out_parts(own_slot(m), ostage.at[m % 4], act)
 
     def lent_out(e, method):
         def act(src, dst, i):
@@ -422,25 +455,25 @@
             )
             getattr(copy, method)()
 
-        out_parts(e * LEND_EVERY + LEND_EVERY - 1, ostage.at[(slots + e) % 4], act)
+        out_parts(e * LEND_EVERY + LEND_EVERY - 1, ostage.at[(lent_from + e) % 4], act)
 
     def out_start(m):
-        @pl.when(m < slots)
+        @pl.when(jnp.logical_not(is_borrowed(m)))
         def _():
             own_out(m, "start")
 
-        @pl.when(m >= slots)
-        def _():
-            lent_out(m - slots, "start")
+        @pl.when(is_borrowed(m))
+        def _():
+            lent_out(m - lent_from, "start")
 
     def out_wait(m):
-        @pl.when(m < slots)
+        @pl.when(jnp.logical_not(is_borrowed(m)))
         def _():
             own_out(m, "wait")
 
-        @pl.when(m >= slots)
-        def _():
-            lent_out(m - slots, "wait_send")
+        @pl.when(is_borrowed(m))
+        def _():
+            lent_out(m - lent_from, "wait_send")
 
     def result_stay():
         return pltpu.make_async_copy(fout.at[aligned(yy * blk, blk)], results.at[yy], res_sem.at[0])
@@ -517,7 +550,7 @@
         take(0, t, RING)
         core_copy(t).start()
 
-        @pl.when(t == slot_at(vslot))
+        @pl.when(t == own_slot(vslot))
         def _():
             vsend[0, :, 0:width] = vec[...]
             vsend[0, :, width : width + 256] = dcf[...]
@@ -526,14 +559,16 @@
         return carry
 
     def stage_chip(p, carry):
-        at = p % RING
+        own = jnp.where(is_first, p, p - lent_before(p))
+        borrowed = is_borrowed(p)
+        at = own % RING
         away = 1 - yy
         t = place_of(p)
         keeps = jnp.logical_not(is_lent(p))
 
-        @pl.when(p < slots)
-        def _():
-            core_copy(p).wait_recv()
+        @pl.when(jnp.logical_not(borrowed))
+        def _():
+            core_copy(own).wait_recv()
 
         @pl.when(keeps)
         def _():
@@ -543,16 +578,16 @@
             def _():
                 y_copy(t - YRING).wait_send()
 
-            @pl.when(p < slots)
+            @pl.when(jnp.logical_not(borrowed))
             def _():
                 ysend[t % YRING] = (ckeep[at, away] + crecv[at, away].astype(F32)).astype(BF)
                 rown[t % OWN_RING] = (ckeep[at, yy] + crecv[at, yy].astype(F32)).astype(BF)
 
-            @pl.when(p >= slots)
-            def _():
-                lend_copy(p - slots).wait_recv()
-                ysend[t % YRING] = lent[p - slots, away]
-                rown[t % OWN_RING] = lent[p - slots, yy]
+            @pl.when(borrowed)
+            def _():
+                lend_copy(p - lent_from).wait_recv()
+                ysend[t % YRING] = lent[p - lent_from, away]
+                rown[t % OWN_RING] = lent[p - lent_from, yy]
 
             y_copy(t).start()
 
@@ -569,9 +604,9 @@
                 lent[e, side] = (ckeep[at, side] + crecv[at, side].astype(F32)).astype(BF)
             lend_copy(e).start()
 
-        @pl.when(p < slots)
-        def _():
-            give(0, p, RING, sib, slots)
+        @pl.when(jnp.logical_not(borrowed))
+        def _():
+            give(0, own, RING, sib, slots)
 
         return carry
 
@@ -682,7 +717,8 @@
         result_stay().start()
         result_move().start()
         own_block(cot).wait()
-        swap_block(cot).wait()
+        swap_half(cot, 0).wait()
+        swap_half(cot, 1).wait()
 
     def scale_back(j):
         part = aligned(j * blk, blk)
@@ -697,15 +733,17 @@
         dmb[part, :] = low
         vec[9:10, :] += jnp.sum(low.astype(F32), 0, keepdims=True)
 
-    def shrink_back(j, t):
+    def shrink_back(j):
         part = aligned(j * blk, blk)
-        cols = aligned(t * width, width)
-        back = dot_nt(dmb[part, :], wfc2[cols, :])
-        low = (gp[part, cols].astype(F32) * back).astype(BF)
-        du[part, cols] = low
-        sums = jnp.sum(low.astype(F32), 0, keepdims=True)
-        for i in range(width // 256):
-            dcf[pl.ds(t * (width // 256) + i, 1), :] += sums[:, i * 256 : (i + 1) * 256]
+        for t in range(ff // width):
+            cols = slice(t * width, (t + 1) * width)
+            back = dot_nt(dmb[part, :], wfc2[cols, :])
+            low = (gp[part, cols].astype(F32) * back).astype(BF)
+            du[part, cols] = low
+            sums = jnp.sum(low.astype(F32), 0, keepdims=True)
+            for i in range(width // 256):
+                row = t * (width // 256) + i
+                dcf[row : row + 1, :] += sums[:, i * 256 : (i + 1) * 256]
 
     def middle_back(j):
         part = aligned(j * blk, blk)
@@ -745,28 +783,44 @@
             device_id_type=MESH,
         )
 
-    def quadrant(keys, values, query, outer):
-        prob = jnp.exp(dot_nt(keys, query))
-        diff = dot_nt(values, outer)
+    def stacked(ref, pair, part):
+        first, second = ref[2 * pair, part], ref[2 * pair + 1, part]
+        return jnp.concatenate(
+            [
+                jnp.concatenate([first * first_row, first * second_row], 1),
+                jnp.concatenate([second * second_row, second * first_row], 1),
+            ],
+            0,
+        )
+
+    def quadrant(pair, j, part):
+        cols = aligned(pair * 128, 128)
+
+        def key_block(ref):
+            return jnp.concatenate(
+                [ref[j * blk : (j + 1) * blk, cols], ref[rows + j * blk : rows + (j + 1) * blk, cols]], 0
+            )
+
+        feats = jnp.concatenate([segf[j * blk : (j + 1) * blk], segf[rows + j * blk : rows + (j + 1) * blk]], 0)
+        keys, values = key_block(kall), key_block(vall)
+        query, outer = stacked(qaug, pair, part), stacked(doaug, pair, part)
+        prob = jnp.exp(dot_nt(jnp.concatenate([keys, feats], 1), query))
+        diff = dot_nt(jnp.concatenate([values, feats], 1), outer)
         slope = (prob * diff).astype(BF)
-        return dot_tn(slope, keys), dot_nn(slope, query), dot_nn(prob.astype(BF), outer)
-
-    def both_heads(parts):
-        return [jnp.where(lane_row < 64, first, second) for first, second in zip(*parts)]
-
-    def key_block(array, j):
-        return jnp.concatenate([array[j * blk : (j + 1) * blk], array[rows + j * blk : rows + (j + 1) * blk]], 0)
+        dq = dot_tn(slope, keys)
+        count = dq.shape[0] // 2
+        return (
+            jnp.where(lane_row < 64, dq[:count], dq[count:]),
+            dot_nn(slope, query[:, 0:128]),
+            dot_nn(prob.astype(BF), outer[:, 0:128]),
+        )
 
     def pair_spans(pair):
         return [aligned(third * width + pair * 128, 128) for third in range(3)]
 
     def attend_back_first(pair):
-        wide, narrow = [], []
-        for i, (keys, values) in enumerate(aug_pair(pair)):
-            query, outer = qaug[2 * pair + i], doaug[2 * pair + i]
-            wide.append(quadrant(key_block(keys, 0), key_block(values, 0), query, outer))
-            narrow.append(quadrant(key_block(keys, 1), key_block(values, 1), query[0:blk], outer[0:blk]))
-        (dq_w, dk_w, dv_w), (dq_n, dk_n, dv_n) = both_heads(wide), both_heads(narrow)
+        dq_w, dk_w, dv_w = quadrant(pair, 0, slice(0, rows))
+        dq_n, dk_n, dv_n = quadrant(pair, 1, slice(0, blk))
         q_cols, k_cols, v_cols = pair_spans(pair)
         dkv_send[pair, 0:blk] = dk_w[blk:].astype(BF)
         dkv_send[pairs + pair, 0:blk] = dv_w[blk:].astype(BF)
@@ -782,16 +836,9 @@
         dqkv[blk:, v_cols] = dv_n[0:blk].astype(BF)
 
     def attend_back_second(duo):
-        found = [second_terms(2 * duo + i) for i in range(2)]
+        found = [quadrant(2 * duo + i, 1, slice(blk, rows)) for i in range(2)]
         for i in range(2):
             second_sums(2 * duo + i, *found[i])
-
-    def second_terms(pair):
-        parts = []
-        for i, (keys, values) in enumerate(aug_pair(pair)):
-            query, outer = qaug[2 * pair + i, blk:], doaug[2 * pair + i, blk:]
-            parts.append(quadrant(key_block(keys, 1), key_block(values, 1), query, outer))
-        return both_heads(parts)
 
     def second_sums(pair, dq, dk, dv):
         q_cols, k_cols, v_cols = pair_spans(pair)
@@ -804,18 +851,17 @@
     def finish_back(j):
         part = aligned(j * blk, blk)
 
-        def collect(index, carry):
+        for index in range(2 * pairs):
             dkv_copy(index, j).wait()
-            cols = aligned(width + index * 128, 128)
+        for index in range(2 * pairs):
+            cols = slice(width + index * 128, width + (index + 1) * 128)
             dqkv[part, cols] = (dqkv[part, cols].astype(F32) + dkv_recv[index, part].astype(F32)).astype(BF)
-            return carry
-
-        lax.fori_loop(0, 2 * pairs, collect, 0)
 
         @pl.when(is_first & (j == 0))
         def _():
-            for i in range(chunks):
-                x_send(hin, fout, i, x_ssem, x_rsem).wait_send()
+            x_send(hin, fout, 0, x_ssem, x_rsem).wait_send()
+            x_half(0).wait_send()
+            x_half(1).wait_send()
 
         @pl.when(is_second & (j == 0))
         def _():
@@ -835,8 +881,7 @@
         def _():
             x_send(cot, dout, j, xb_ssem, xb_rsem).start()
 
-    tiles = ff // width
-    per_block = tiles + 3
+    per_block = 4
     dense = chunks * per_block
     first_end = dense + pairs
     second_end = first_end + 1 + pairs // 2
@@ -868,15 +913,15 @@
             def _():
                 scale_back(j)
 
-            @pl.when((r > 0) & (r <= tiles))
-            def _():
-                shrink_back(j, r - 1)
-
-            @pl.when(r == tiles + 1)
+            @pl.when(r == 1)
+            def _():
+                shrink_back(j)
+
+            @pl.when(r == 2)
             def _():
                 middle_back(j)
 
-            @pl.when(r == tiles + 2)
+            @pl.when(r == 3)
             def _():
                 heads_back(j)
 
@@ -896,7 +941,7 @@
 
     def visit(v, carry):
         lax.fori_loop(pieces_done(v - 1), pieces_done(v), piece, 0)
-        advance(stage_own, 0, jnp.minimum(mine, slots), v, slot_at)
+        advance(stage_own, 0, mine, v, own_slot)
         advance(stage_chip, chip_lag, mine, v, slot_at)
         advance(stage_group, group_lag, mine, v)
         for way in range(2):
@@ -1290,7 +1335,7 @@
         bf(keys, 128), f32(RING, 2, *slot), bf(RING, 2, *slot), bf(RING, 2, *slot),
         bf(YRING, *slot), bf(YRING, *slot), bf(OWN_RING, *slot), bf(2, RING, *slot), bf(2, ZRING, *slot), bf(4, *slot),
         f32(16, width), f32(16, 256), f32(5, 16, width + 256), f32(4, 16, width + 256), bf(LENT, 2, *slot),
-        dma((4,)), dma(()), dma((2,)), dma((2, 2)), dma((2, 2)), dma((2,)), dma((2,)), dma((2,)), dma((2,)),
+        dma((4,)), dma(()), dma((2, 2)), dma((2, 4)), dma((2, 4)), dma((3,)), dma((3,)), dma((2,)), dma((2,)),
         dma((heads, 2)), dma((heads, 2)), dma((3,)),
         dma((RING,)), dma((RING,)), dma((YRING,)), dma((YRING,)), dma((2, RING)), dma((2, ZRING)), dma((4, 2)),
         dma((4,)), dma((4,)), dma((3 * LENT,)), dma((3 * LENT,)), pltpu.SemaphoreType.REGULAR((4,)),
@@ -1344,7 +1389,7 @@
 
 
 def widen(results, qkv, proj, fc1, fc2, vecs):
-    steps = 4
+    steps = 2
 
     def block(shape, lead):
         size = (shape[0] // steps,) + shape[1:]

time: 238 us -> 222 us (0.933)
  Pallas kernels: 237 us -> 220 us
    pallas_call x1, Pallas kernels: 231 us -> 215 us  [fused_body(): pl.pallas_call(functools.partial(kernel, groups), out_shape=(jax.ShapeDty...]
where the time goes in v1:
time: 222 us; the launch traced here: 221 us
  Pallas kernels  220 us (99%)
    pallas_call x1, Pallas kernels, fused_body(): pl.pallas_call(functools.partial(kernel, groups), out_shape=(jax.ShapeDty...  215 us
    pallas_call x1, Pallas kernels, widen(): pl.pallas_call(widen_kernel, grid=(steps,), in_specs=[block(a.shape, Fals...  5.27 us

profile of v1, /device:TPU:0, one launch (start us, length us, event | category | flops | bytes accessed | tf_op | source)
XLA Modules:
  0.0 221.3 jit_solution(256222548476321816)
XLA Ops:
  0.6 215.2 %two_layers.1 = (bf16[2,256,768]{2,1,0:T(8,128)(2,1)}, bf16[192,2304]{1,0:T(8,128)(2,1)}, bf16[192,768]{1,0:T(8,128)(2,1)}, bf16[192,3072]{1,0:T(8,128)(2,1)}, b...) custom-call(bf16[1,2,256,768]{3,2,1,0:T(8,128)(2,1)} %refs_0_.1, s32[2,1024]{1,0:T(2,128)} %refs_1_.1, ...), custom_call_target="tpu_custom_call" | custom-call | tf_op jit(solution)/shard_map/two_layers/pallas_call | solution.py:1345
  215.9 5.3 %widen.1 = (bf16[1,512,768]{2,1,0:T(8,128)(2,1)}, f32[1,192,2304]{2,1,0:T(8,128)}, f32[1,192,768]{2,1,0:T(8,128)}, f32[1,192,3072]{2,1,0:T(8,128)}, f32[1,768,76...) custom-call(bf16[512,768]{1,0:T(8,128)(2,1)} %bitcast.4, ...), custom_call_target="tpu_custom_call" | custom-call | tf_op jit(solution)/shard_map/widen/pallas_call | solution.py:1409

commit v2 on v1

--- a/solution.py
+++ b/solution.py
@@ -16,7 +16,7 @@
 ZRING = 8
 YRING = 6
 OWN_RING = 12
-LENT = 5
+LENT = 6
 LEND_EVERY = 5
 BF = jnp.bfloat16
 F32 = jnp.float32
@@ -197,12 +197,12 @@
         )
 
     def x_half(half):
-        part = aligned((chunks - 1) * blk + half * half_blk, half_blk)
+        part = aligned(half * half_blk, half_blk)
         return pltpu.make_async_remote_copy(
             src_ref=fout.at[part],
             dst_ref=hin.at[part],
-            send_sem=x_ssem.at[chunks - 1 + half],
-            recv_sem=x_rsem.at[chunks - 1 + half],
+            send_sem=x_ssem.at[half],
+            recv_sem=x_rsem.at[half],
             device_id=xnb,
             device_id_type=MESH,
         )
@@ -235,35 +235,31 @@
             qaug[2 * i, part, :] = jnp.where(lane_row < 64, pair, penalty).astype(BF)
             qaug[2 * i + 1, part, :] = jnp.where(lane_row < 64, penalty, pair).astype(BF)
 
+    first_at = jnp.where(is_first, yy, 0) * blk
+
     @pl.when(is_first)
     def _():
         own_block(hin).wait()
 
-    @pl.when(is_second)
-    def _():
-        x_send(hin, fout, 0, x_ssem, x_rsem).wait_recv()
-
     weight_copies[0].wait()
-    first_at = jnp.where(is_first, yy, 0) * blk
-    project(aligned(first_at, blk))
 
     def project_half(half, carry):
-        @pl.when(is_first)
-        def _():
-            swap_half(hin, half).wait()
+        @pl.when(is_first & (half >= 2))
+        def _():
+            swap_half(hin, half % 2).wait()
 
         @pl.when(is_second)
         def _():
             x_half(half).wait_recv()
 
-        project(aligned(blk - first_at + half * half_blk, half_blk))
+        start = jnp.where(half < 2, first_at, blk - first_at) + (half % 2) * half_blk
+        project(aligned(start, half_blk))
         return carry
 
-    lax.fori_loop(0, 2, project_half, 0)
+    lax.fori_loop(0, 4, project_half, 0)
     for which in range(2):
-        kv_copy(which, aligned(first_at, blk)).wait()
-        for half in range(2):
-            kv_copy(which, aligned(blk - first_at + half * half_blk, half_blk)).wait()
+        for half in range(4):
+            kv_copy(which, aligned(half * half_blk, half_blk)).wait()
 
     def feed_forward(part):
         branch = dot_nn(ob[part, :], wproj[...]) + bias(3)
@@ -328,22 +324,18 @@
             for copy in weight_copies[1:]:
                 copy.wait()
 
-        @pl.when(is_first & (j == chunks - 1))
+        @pl.when(is_first)
         def _():
             def feed_half(half, carry):
-                feed_forward(aligned((chunks - 1) * blk + half * half_blk, half_blk))
+                feed_forward(aligned(half * half_blk, half_blk))
                 x_half(half).start()
                 return carry
 
-            lax.fori_loop(0, 2, feed_half, 0)
-
-        @pl.when(is_second | (j < chunks - 1))
+            lax.fori_loop(2 * j, 2 * j + 2, feed_half, 0)
+
+        @pl.when(is_second)
         def _():
             feed_forward(part)
-
-        @pl.when(is_first & (j < chunks - 1))
-        def _():
-            x_send(hin, fout, j, x_ssem, x_rsem).start()
 
         return carry
 
@@ -358,7 +350,7 @@
     lo_qkv = lo_proj + n_proj
     slots = lo_qkv + n_qkv
     mine = jnp.where(is_first, slots - LENT, slots + LENT)
-    vslot = slots - LENT - 4
+    vslot = slots - LENT - 6
     lent_from = slots - LENT - 1
 
     def slot_at(m):
@@ -616,7 +608,7 @@
         rown[at] = (rown[at].astype(F32) + yrecv[t % YRING].astype(F32)).astype(BF)
         give(1, t, YRING, ynb)
 
-        @pl.when(t == vslot)
+        @pl.when(t == vslot + 1)
         def _():
             v_copy(1, ynb).wait()
             vsend[2] = vsend[1] + vrecv[1]
@@ -653,7 +645,7 @@
 
             z_copy(way, t).start()
 
-        @pl.when(t == vslot)
+        @pl.when(t == vslot + 1 + (grp if way == 0 else groups - 1 - grp))
         def _():
             @pl.when(has_before)
             def _():
@@ -859,27 +851,27 @@
 
         @pl.when(is_first & (j == 0))
         def _():
-            x_send(hin, fout, 0, x_ssem, x_rsem).wait_send()
-            x_half(0).wait_send()
-            x_half(1).wait_send()
+            for half in range(4):
+                x_half(half).wait_send()
 
         @pl.when(is_second & (j == 0))
         def _():
             result_stay().wait()
             result_move().wait_send()
 
+        grad_one = dot_nt(dqkv[part, :], wqkv[...])
+        hat, rstd = norm_stats(hin[part, :].astype(F32))
+        total = drb[part, :] + norm_back(grad_one, hat, rstd, gains[0, 0:1, :])
+        dout[part, :] = total.astype(BF)
+
+        @pl.when(is_second)
+        def _():
+            x_send(cot, dout, j, xb_ssem, xb_rsem).start()
+
+        vec[0:1, :] += jnp.sum(grad_one * hat, 0, keepdims=True)
+        vec[4:5, :] += jnp.sum(grad_one, 0, keepdims=True)
         vec[5:6, :] += jnp.sum(dqkv[part, 0:width].astype(F32), 0, keepdims=True)
         vec[6:7, :] += jnp.sum(dqkv[part, 2 * width : 3 * width].astype(F32), 0, keepdims=True)
-        grad_one = dot_nt(dqkv[part, :], wqkv[...])
-        hat, rstd = norm_stats(hin[part, :].astype(F32))
-        vec[0:1, :] += jnp.sum(grad_one * hat, 0, keepdims=True)
-        vec[4:5, :] += jnp.sum(grad_one, 0, keepdims=True)
-        total = drb[part, :] + norm_back(grad_one, hat, rstd, gains[0, 0:1, :])
-        dout[part, :] = total.astype(BF)
-
-        @pl.when(is_second)
-        def _():
-            x_send(cot, dout, j, xb_ssem, xb_rsem).start()
 
     per_block = 4
     dense = chunks * per_block
@@ -949,7 +941,7 @@
             advance(functools.partial(stage_line, way), group_lag + hop_lag * place, mine, v)
         advance(stage_whole, group_lag + hop_lag * late, mine, v)
 
-        @pl.when(is_first & (v == slots))
+        @pl.when(is_first & (v == mine + 1))
         def _():
             result_stay().start()
             result_move().start()
@@ -1335,7 +1327,7 @@
         bf(keys, 128), f32(RING, 2, *slot), bf(RING, 2, *slot), bf(RING, 2, *slot),
         bf(YRING, *slot), bf(YRING, *slot), bf(OWN_RING, *slot), bf(2, RING, *slot), bf(2, ZRING, *slot), bf(4, *slot),
         f32(16, width), f32(16, 256), f32(5, 16, width + 256), f32(4, 16, width + 256), bf(LENT, 2, *slot),
-        dma((4,)), dma(()), dma((2, 2)), dma((2, 4)), dma((2, 4)), dma((3,)), dma((3,)), dma((2,)), dma((2,)),
+        dma((4,)), dma(()), dma((2, 2)), dma((2, 4)), dma((2, 4)), dma((4,)), dma((4,)), dma((2,)), dma((2,)),
         dma((heads, 2)), dma((heads, 2)), dma((3,)),
         dma((RING,)), dma((RING,)), dma((YRING,)), dma((YRING,)), dma((2, RING)), dma((2, ZRING)), dma((4, 2)),
         dma((4,)), dma((4,)), dma((3 * LENT,)), dma((3 * LENT,)), pltpu.SemaphoreType.REGULAR((4,)),

time: 222 us -> 221 us (level)
    pallas_call x1, Pallas kernels: 215 us -> 212 us  [fused_body(): pl.pallas_call(functools.partial(kernel, groups), out_shape=(jax.ShapeDty...]
where the time goes in v2:
time: 221 us; the launch traced here: 218 us
  Pallas kernels  218 us (99%)
    pallas_call x1, Pallas kernels, fused_body(): pl.pallas_call(functools.partial(kernel, groups), out_shape=(jax.ShapeDty...  212 us
    pallas_call x1, Pallas kernels, widen(): pl.pallas_call(widen_kernel, grid=(steps,), in_specs=[block(a.shape, Fals...  5.27 us

profile of v2, /device:TPU:0, one launch (start us, length us, event | category | flops | bytes accessed | tf_op | source)
XLA Modules:
  0.0 218.5 jit_solution(11693195793698256314)
XLA Ops:
  0.6 212.4 %two_layers.1 = (bf16[2,256,768]{2,1,0:T(8,128)(2,1)}, bf16[192,2304]{1,0:T(8,128)(2,1)}, bf16[192,768]{1,0:T(8,128)(2,1)}, bf16[192,3072]{1,0:T(8,128)(2,1)}, b...) custom-call(bf16[1,2,256,768]{3,2,1,0:T(8,128)(2,1)} %refs_0_.1, s32[2,1024]{1,0:T(2,128)} %refs_1_.1, ...), custom_call_target="tpu_custom_call" | custom-call | tf_op jit(solution)/shard_map/two_layers/pallas_call | solution.py:1337
  213.1 5.3 %widen.1 = (bf16[1,512,768]{2,1,0:T(8,128)(2,1)}, f32[1,192,2304]{2,1,0:T(8,128)}, f32[1,192,768]{2,1,0:T(8,128)}, f32[1,192,3072]{2,1,0:T(8,128)}, f32[1,768,76...) custom-call(bf16[512,768]{1,0:T(8,128)(2,1)} %bitcast.4, ...), custom_call_target="tpu_custom_call" | custom-call | tf_op jit(solution)/shard_map/widen/pallas_call | solution.py:1401

commit v3 on v2

--- a/solution.py
+++ b/solution.py
@@ -502,7 +502,7 @@
 
                 @pl.when(cc == dest % 2)
                 def _():
-                    place(ckeep, F32)
+                    place(ckeep, BF)
 
                 @pl.when(cc != dest % 2)
                 def _():
@@ -527,7 +527,7 @@
                             mine, theirs = slice(0, SLOT_ROWS), slice(SLOT_ROWS, 2 * SLOT_ROWS)
                             if core:
                                 mine, theirs = theirs, mine
-                            ckeep[ring + i, side] = got[mine, span]
+                            ckeep[ring + i, side] = got[mine, span].astype(BF)
                             csend[ring + i, side] = got[theirs, span].astype(BF)
 
                 return carry
@@ -572,8 +572,8 @@
 
             @pl.when(jnp.logical_not(borrowed))
             def _():
-                ysend[t % YRING] = (ckeep[at, away] + crecv[at, away].astype(F32)).astype(BF)
-                rown[t % OWN_RING] = (ckeep[at, yy] + crecv[at, yy].astype(F32)).astype(BF)
+                ysend[t % YRING] = (ckeep[at, away].astype(F32) + crecv[at, away].astype(F32)).astype(BF)
+                rown[t % OWN_RING] = (ckeep[at, yy].astype(F32) + crecv[at, yy].astype(F32)).astype(BF)
 
             @pl.when(borrowed)
             def _():
@@ -593,7 +593,7 @@
         def _():
             e = p // LEND_EVERY
             for side in range(2):
-                lent[e, side] = (ckeep[at, side] + crecv[at, side].astype(F32)).astype(BF)
+                lent[e, side] = (ckeep[at, side].astype(F32) + crecv[at, side].astype(F32)).astype(BF)
             lend_copy(e).start()
 
         @pl.when(jnp.logical_not(borrowed))
@@ -1324,7 +1324,7 @@
         bf(keys, width), bf(keys, width), bf(rows, width), f32(rows, width),
         bf(rows, ff + 4 * width), bf(rows, ff), bf(rows, width), bf(rows, width),
         bf(rows, width), bf(heads, rows, 128), bf(heads, rows, 128), bf(heads, rows, 128),
-        bf(keys, 128), f32(RING, 2, *slot), bf(RING, 2, *slot), bf(RING, 2, *slot),
+        bf(keys, 128), bf(RING, 2, *slot), bf(RING, 2, *slot), bf(RING, 2, *slot),
         bf(YRING, *slot), bf(YRING, *slot), bf(OWN_RING, *slot), bf(2, RING, *slot), bf(2, ZRING, *slot), bf(4, *slot),
         f32(16, width), f32(16, 256), f32(5, 16, width + 256), f32(4, 16, width + 256), bf(LENT, 2, *slot),
         dma((4,)), dma(()), dma((2, 2)), dma((2, 4)), dma((2, 4)), dma((4,)), dma((4,)), dma((2,)), dma((2,)),

time: 221 us -> 221 us (level)
  no operation moved by 1% of the time
where the time goes in v3:
time: 221 us; the launch traced here: 219 us
  Pallas kernels  218 us (99%)
    pallas_call x1, Pallas kernels, fused_body(): pl.pallas_call(functools.partial(kernel, groups), out_shape=(jax.ShapeDty...  213 us
    pallas_call x1, Pallas kernels, widen(): pl.pallas_call(widen_kernel, grid=(steps,), in_specs=[block(a.shape, Fals...  5.27 us

profile of v3, /device:TPU:0, one launch (start us, length us, event | category | flops | bytes accessed | tf_op | source)
XLA Modules:
  0.0 218.7 jit_solution(11731571306455709913)
XLA Ops:
  0.6 212.6 %two_layers.1 = (bf16[2,256,768]{2,1,0:T(8,128)(2,1)}, bf16[192,2304]{1,0:T(8,128)(2,1)}, bf16[192,768]{1,0:T(8,128)(2,1)}, bf16[192,3072]{1,0:T(8,128)(2,1)}, b...) custom-call(bf16[1,2,256,768]{3,2,1,0:T(8,128)(2,1)} %refs_0_.1, s32[2,1024]{1,0:T(2,128)} %refs_1_.1, ...), custom_call_target="tpu_custom_call" | custom-call | tf_op jit(solution)/shard_map/two_layers/pallas_call | solution.py:1337
  213.3 5.3 %widen.1 = (bf16[1,512,768]{2,1,0:T(8,128)(2,1)}, f32[1,192,2304]{2,1,0:T(8,128)}, f32[1,192,768]{2,1,0:T(8,128)}, f32[1,192,3072]{2,1,0:T(8,128)}, f32[1,768,76...) custom-call(bf16[512,768]{1,0:T(8,128)(2,1)} %bitcast.4, ...), custom_call_target="tpu_custom_call" | custom-call | tf_op jit(solution)/shard_map/widen/pallas_call | solution.py:1401
